TPU v7x, 32 devices: a whole 2x2x4 slice. The times are simulated.
32 devices in a mesh: group: 2 (over x), strike: 16 (over z, y, core).
Axes of the slice: x: 2, y: 2, z: 4, core: 2. Of those that a mesh axis runs over, the one named last changes fastest.
Arguments:
- pressure: float32 [128, 8, 512], P(('group', 'strike')), parts along dimension 0, may hold values from -4 to 4
- newton_step: float32 [128, 8, 512], P(('group', 'strike')), parts along dimension 0, may hold values from -4 to 4
- pore_volume: float32 [128, 8, 512], P(('group', 'strike')), parts along dimension 0, may hold values from 0.5 to 4
- old_mass: float32 [128, 8, 512], P(('group', 'strike')), parts along dimension 0, may hold values from 0.5 to 3
- trans_strike: float32 [128, 8, 512], P(('group', 'strike')), parts along dimension 0, may hold values from 0.05 to 1
- trans_layer: float32 [128, 8, 512], P(('group', 'strike')), parts along dimension 0, may hold values from 0.05 to 1
- trans_dip: float32 [128, 8, 512], P(('group', 'strike')), parts along dimension 0, may hold values from 0.05 to 1
- frac_pressure: float32 [32, 128, 128], P(('group', 'strike')), parts along dimension 0, may hold values from -4 to 4
- frac_step: float32 [32, 128, 128], P(('group', 'strike')), parts along dimension 0, may hold values from -4 to 4
- frac_volume: float32 [32, 128, 128], P(('group', 'strike')), parts along dimension 0, may hold values from 0.2 to 2
- frac_old_mass: float32 [32, 128, 128], P(('group', 'strike')), parts along dimension 0, may hold values from 0.2 to 2
- frac_trans_along: float32 [32, 128, 128], P(('group', 'strike')), parts along dimension 0, may hold values from 0.3 to 4
- frac_trans_across: float32 [32, 128, 128], P(('group', 'strike')), parts along dimension 0, may hold values from 0.3 to 4
- conn_count: int32 [32, 16], P(('group', 'strike')), parts along dimension 0, may hold values from 1 to 32, as said below
- conn_trans: float32 [32, 16, 32], P(('group', 'strike')), parts along dimension 0, may hold values from 0.1 to 2
- frac_index: int32 [32, 16, 32], P(('group', 'strike')), parts along dimension 0, may hold values from 0 to 16383
- matrix_index: int32 [32, 16, 32], P(('group', 'strike')), parts along dimension 0, may hold values from 0 to 16383
Outputs:
- matrix_residual: float32 [128, 8, 512], P(('group', 'strike')), parts along dimension 0
- matrix_product: float32 [128, 8, 512], P(('group', 'strike')), parts along dimension 0
- fracture_residual: float32 [32, 128, 128], P(('group', 'strike')), parts along dimension 0
- fracture_product: float32 [32, 128, 128], P(('group', 'strike')), parts along dimension 0
There are 2 independent parts, one for each index of `group`. A program takes and returns all parts, laid end to end along the dimension named above; each array names one. Nothing has to cross between parts.
Inputs may be any that keep to these rules, and one draw needn't show every extreme that they name: In every part one strike index d is drawn for which conn_count[s, d] = 32 for every s; the other counts are even over the range.
All inputs are finite; a program needn't handle non-finite values.
Results may differ from a plain program's by a relative error of at most 0.0003.
Values sent between devices are 32-bit elements; how exact they have to be, the bound alone decides.
A program may use at most 64 MiB of HBM per device.

v0:
```python
import functools

import jax
import jax.numpy as jnp
from jax import lax
from jax.experimental import pallas as pl
from jax.experimental.pallas import tpu as pltpu
from jax.sharding import PartitionSpec as P

COMPRESSIBILITY = 0.5
LANES = 128
MESH = pl.DeviceIdType.MESH


def face(trans, pa, pb, da, db, ea, eb, ga, gb):
    drop = pa - pb
    total = 0.5 * trans * (ea + eb)
    flux = total * drop
    tangent = (0.25 * trans) * (ga + gb) * drop + total * (da - db)
    return flux, tangent


def shift_faces(resid, linear, trans, p, d, e, g, axis):
    size = p.shape[axis]
    here = lax.broadcasted_iota(jnp.int32, p.shape, axis)
    trans = jnp.where(here < size - 1, trans, 0.0)
    up = lambda x: pltpu.roll(x, size - 1, axis)
    down = lambda x: pltpu.roll(x, 1, axis)
    flux, tangent = face(trans, p, up(p), d, up(d), e, up(e), g, up(g))
    return resid + flux - down(flux), linear + tangent - down(tangent)


def split(x, terms):
    out = []
    for _ in range(terms):
        head = x.astype(jnp.bfloat16)
        out.append(head)
        x = x - head.astype(jnp.float32)
    return out


def pack(x):
    fold = LANES // x.shape[1]
    n = x.shape[0] // fold
    return jnp.concatenate([x[b * n : (b + 1) * n] for b in range(fold)], axis=1)


def unpack(x, width):
    fold = LANES // width
    return jnp.concatenate([x[:, b * width : (b + 1) * width] for b in range(fold)], axis=0)


def wide(rows, ref_rows):
    iota = lax.broadcasted_iota(jnp.int32, (ref_rows, LANES), 0)
    return [iota == rows[a : a + 1, :] for a in range(rows.shape[0])]


def ones_of(masks):
    return jnp.concatenate(
        [jnp.where(m, 1.0, 0.0).astype(jnp.bfloat16) for m in masks], axis=1
    )


def gather(first, second, row_masks, col_ones):
    size = first.shape[0]
    lhs = jnp.concatenate(
        [jnp.concatenate(split(x, 3), axis=1) for x in (first, second)], axis=0
    )
    rhs = jnp.concatenate([col_ones] * 3, axis=0)
    found = jnp.dot(lhs, rhs, preferred_element_type=jnp.float32)
    out = []
    for q in range(2):
        rows = []
        for a, mask in enumerate(row_masks):
            block = found[q * size : (q + 1) * size, a * LANES : (a + 1) * LANES]
            rows.append(jnp.sum(jnp.where(mask, block, 0.0), axis=0, keepdims=True))
        out.append(jnp.concatenate(rows, axis=0))
    return out


def scatter(first, second, row_ones, col_masks):
    def weights(part):
        stacked = []
        for rows in part:
            stacked.append(
                jnp.concatenate(
                    [
                        jnp.where(mask, rows[a : a + 1, :].astype(jnp.float32), 0.0).astype(
                            jnp.bfloat16
                        )
                        for a, mask in enumerate(col_masks)
                    ],
                    axis=1,
                )
            )
        return jnp.concatenate(stacked, axis=1)

    rhs = jnp.concatenate([weights(split(first, 2)), weights(split(second, 2))], axis=0)
    lhs = jnp.concatenate([row_ones] * 2, axis=1)
    sums = lax.dot_general(
        lhs, rhs, (((1,), (1,)), ((), ())), preferred_element_type=jnp.float32
    )
    return sums[:, :LANES], sums[:, LANES:]


def store(*refs):
    n = (len(refs) - 1) // 2
    copies = [
        pltpu.make_async_copy(refs[i], refs[n + i], refs[-1].at[i]) for i in range(n)
    ]
    for copy in copies:
        copy.start()
    for copy in copies:
        copy.wait()


def kernel(peers, *refs):
    ins, outs, scratch = refs[:17], refs[17:21], refs[21:]
    bufs = scratch[:17]
    send, recv, low, high, load_sem, send_sem, recv_sem, halo_send, halo_recv = scratch[17:]
    me = lax.axis_index("strike")
    load = [
        pltpu.make_async_copy(ins[i], bufs[i], load_sem.at[i]) for i in range(17)
    ]
    order = (16, 15, 0, 1, 7, 8, 13, 14, 2, 3, 4, 5, 6, 9, 10, 11, 12)
    for i in order:
        load[i].start()

    barrier = pltpu.get_barrier_semaphore()

    def greet(off, carry):
        pl.semaphore_signal(
            barrier, 1, device_id={"strike": lax.rem(me + off, peers)}, device_id_type=MESH
        )
        return carry

    lax.fori_loop(1, peers, greet, 0, unroll=peers <= 16)

    (press, step, pore, old, t_strike, t_layer, t_dip) = bufs[:7]
    (f_press, f_step, f_volume, f_old, f_along, f_across) = bufs[7:13]
    count, c_trans, f_index, m_index = bufs[13:]
    nx, nz, ny = press.shape
    side = f_press.shape[1]
    rows_m = nx * nz
    cols = ny // LANES
    cap = c_trans.shape[2]

    def fold(x):
        flat = x.reshape(rows_m, ny)
        return jnp.concatenate(
            [flat[:, j * LANES : (j + 1) * LANES] for j in range(cols)], axis=0
        )

    def unfold(x):
        flat = jnp.concatenate(
            [x[j * rows_m : (j + 1) * rows_m] for j in range(cols)], axis=1
        )
        return flat.reshape(nx, nz, ny)

    for i in (16, 0, 1):
        load[i].wait()
    cell = pack(m_index[0])
    along = cell & (ny - 1)
    m_row = (along >> 7) * rows_m + (cell >> (ny.bit_length() - 1))
    m_col = along & (LANES - 1)
    m_row_masks = wide(m_row, rows_m * cols)
    m_col_masks = wide(m_col, LANES)
    mp, md = gather(fold(press[...]), fold(step[...]), m_row_masks, ones_of(m_col_masks))
    mp, md = unpack(mp, cap), unpack(md, cap)

    for i in (15, 7, 8):
        load[i].wait()
    cell = pack(f_index[0])
    f_row = cell >> 7
    f_col = cell & (LANES - 1)
    f_row_masks = wide(f_row, side)
    f_col_masks = wide(f_col, LANES)
    fp, fd = gather(f_press[0], f_step[0], f_row_masks, ones_of(f_col_masks))
    fp, fd = unpack(fp, cap), unpack(fd, cap)

    for i in (13, 14):
        load[i].wait()
    diagonal = lax.broadcasted_iota(jnp.int32, (peers, peers), 0) == lax.broadcasted_iota(
        jnp.int32, (peers, peers), 1
    )
    limit = jnp.sum(
        jnp.where(diagonal, count[...].astype(jnp.float32), 0.0), axis=1, keepdims=True
    )
    slot = lax.broadcasted_iota(jnp.int32, (peers, cap), 1).astype(jnp.float32)
    tr = jnp.where(slot < limit, c_trans[0], 0.0)

    first = jnp.concatenate([fp, fd, tr, mp], axis=1)
    send[:, 0, :] = first
    send[:, 1, :] = jnp.concatenate([md, jnp.zeros((peers, LANES - cap), jnp.float32)], axis=1)

    pl.semaphore_wait(barrier, peers - 1)

    def exchange(off, to, slot_there):
        return pltpu.make_async_remote_copy(
            src_ref=send.at[to],
            dst_ref=recv.at[slot_there],
            send_sem=send_sem.at[off],
            recv_sem=recv_sem.at[off],
            device_id={"strike": to},
            device_id_type=MESH,
        )

    def push(off, carry):
        exchange(off, lax.rem(me + off, peers), me).start()
        return carry

    lax.fori_loop(1, peers, push, 0, unroll=peers <= 16)

    following = lax.rem(me + 1, peers)
    previous = lax.rem(me + peers - 1, peers)

    load[4].wait()
    upward = [
        pltpu.make_async_remote_copy(
            src_ref=x.at[nx - 1],
            dst_ref=low.at[i],
            send_sem=halo_send.at[i],
            recv_sem=halo_recv.at[i],
            device_id={"strike": following},
            device_id_type=MESH,
        )
        for i, x in enumerate((press, step, t_strike))
    ]
    downward = [
        pltpu.make_async_remote_copy(
            src_ref=x.at[0],
            dst_ref=high.at[i],
            send_sem=halo_send.at[3 + i],
            recv_sem=halo_recv.at[3 + i],
            device_id={"strike": previous},
            device_id_type=MESH,
        )
        for i, x in enumerate((press, step))
    ]

    @pl.when(me < peers - 1)
    def _():
        for copy in upward:
            copy.start()

    @pl.when(me > 0)
    def _():
        for copy in downward:
            copy.start()

    recv[me] = send[me]

    for i in (2, 3, 5, 6, 9, 10, 11, 12):
        load[i].wait()

    out_mr, out_mp, out_fr, out_fp = outs
    p, d = press[...], step[...]
    e = jnp.exp(COMPRESSIBILITY * p)
    g = e * d
    resid = pore[...] * e - old[...]
    linear = pore[...] * COMPRESSIBILITY * g
    for axis, trans in ((1, t_layer), (2, t_dip)):
        resid, linear = shift_faces(resid, linear, trans[...], p, d, e, g, axis)
    planes_r = [resid[i] for i in range(nx)]
    planes_l = [linear[i] for i in range(nx)]
    for i in range(nx - 1):
        flux, tangent = face(
            t_strike[i], p[i], p[i + 1], d[i], d[i + 1], e[i], e[i + 1], g[i], g[i + 1]
        )
        planes_r[i] = planes_r[i] + flux
        planes_l[i] = planes_l[i] + tangent
        planes_r[i + 1] = planes_r[i + 1] - flux
        planes_l[i + 1] = planes_l[i + 1] - tangent
    for i in range(nx):
        out_mr[i] = planes_r[i]
        out_mp[i] = planes_l[i]

    q, w = f_press[0], f_step[0]
    h = jnp.exp(COMPRESSIBILITY * q)
    k = h * w
    f_resid = f_volume[0] * h - f_old[0]
    f_linear = f_volume[0] * COMPRESSIBILITY * k
    for axis, trans in ((0, f_along), (1, f_across)):
        f_resid, f_linear = shift_faces(f_resid, f_linear, trans[0], q, w, h, k, axis)
    out_fr[0] = f_resid
    out_fp[0] = f_linear

    def edge(trans, a, b):
        return face(
            trans,
            a[0],
            b[0],
            a[1],
            b[1],
            jnp.exp(COMPRESSIBILITY * a[0]),
            jnp.exp(COMPRESSIBILITY * b[0]),
            jnp.exp(COMPRESSIBILITY * a[0]) * a[1],
            jnp.exp(COMPRESSIBILITY * b[0]) * b[1],
        )

    @pl.when(me > 0)
    def _():
        for copy in upward:
            copy.wait_recv()
        flux, tangent = edge(low[2], (low[0], low[1]), (press[0], step[0]))
        out_mr[0] = out_mr[0] - flux
        out_mp[0] = out_mp[0] - tangent

    @pl.when(me < peers - 1)
    def _():
        for copy in downward:
            copy.wait_recv()
        flux, tangent = edge(
            t_strike[nx - 1], (press[nx - 1], step[nx - 1]), (high[0], high[1])
        )
        out_mr[nx - 1] = out_mr[nx - 1] + flux
        out_mp[nx - 1] = out_mp[nx - 1] + tangent

    def take(off, carry):
        exchange(off, lax.rem(me + off, peers), lax.rem(me + peers - off, peers)).wait_recv()
        return carry

    lax.fori_loop(1, peers, take, 0, unroll=peers <= 16)

    got = recv[:, 0, :]
    got_fp, got_fd, got_tr, got_mp = (got[:, i * cap : (i + 1) * cap] for i in range(4))
    got_md = recv[:, 1, 0:cap]

    def link(trans, a, b):
        ea, eb = jnp.exp(COMPRESSIBILITY * a[0]), jnp.exp(COMPRESSIBILITY * b[0])
        return face(trans, a[0], b[0], a[1], b[1], ea, eb, ea * a[1], eb * b[1])

    m_flux, m_tangent = link(got_tr, (mp, md), (got_fp, got_fd))
    sums = scatter(pack(m_flux), pack(m_tangent), ones_of(m_row_masks), m_col_masks)
    out_mr[...] += unfold(sums[0])
    out_mp[...] += unfold(sums[1])
    f_flux, f_tangent = link(tr, (got_mp, got_md), (fp, fd))
    sums = scatter(pack(f_flux), pack(f_tangent), ones_of(f_row_masks), f_col_masks)
    out_fr[0] -= sums[0]
    out_fp[0] -= sums[1]

    def sent(off, carry):
        exchange(off, lax.rem(me + off, peers), me).wait_send()
        return carry

    lax.fori_loop(1, peers, sent, 0, unroll=peers <= 16)

    @pl.when(me < peers - 1)
    def _():
        for copy in upward:
            copy.wait_send()

    @pl.when(me > 0)
    def _():
        for copy in downward:
            copy.wait_send()


def per_device(peers, *args):
    nx, nz, ny = args[0].shape
    sems = lambda n: pltpu.SemaphoreType.DMA((n,))
    outs = [jax.ShapeDtypeStruct(args[i].shape, jnp.float32) for i in (0, 0, 7, 7)]
    spec = lambda space, n: [pl.BlockSpec(memory_space=space)] * n
    args = [pltpu.with_memory_space_constraint(x, pltpu.HBM) for x in args]
    results = pl.pallas_call(
        functools.partial(kernel, peers),
        out_shape=outs,
        in_specs=spec(pltpu.HBM, 17),
        out_specs=spec(pltpu.VMEM, 4),
        scratch_shapes=[pltpu.VMEM(x.shape, x.dtype) for x in args]
        + [
            pltpu.VMEM((peers, 2, LANES), jnp.float32),
            pltpu.VMEM((peers, 2, LANES), jnp.float32),
            pltpu.VMEM((3, nz, ny), jnp.float32),
            pltpu.VMEM((2, nz, ny), jnp.float32),
            sems(17),
            sems(peers),
            sems(peers),
            sems(5),
            sems(5),
        ],
        compiler_params=pltpu.CompilerParams(
            collective_id=0, has_side_effects=True, vmem_limit_bytes=32 * 1024 * 1024
        ),
    )(*args)
    return pl.pallas_call(
        store,
        out_shape=outs,
        in_specs=spec(pltpu.VMEM, 4),
        out_specs=spec(pltpu.HBM, 4),
        scratch_shapes=[sems(4)],
    )(*results)


def solution(mesh):
    three = P(("group", "strike"), None, None)
    two = P(("group", "strike"), None)
    return jax.shard_map(
        functools.partial(per_device, mesh.shape["strike"]),
        mesh=mesh,
        in_specs=(three,) * 13 + (two,) + (three,) * 3,
        out_specs=(three,) * 4,
        check_vma=False,
    )
```

profile of v0, /device:TPU:0, one launch (start us, length us, event | category | flops | bytes accessed | tf_op | source)
XLA Modules:
  0.0 15.6 jit_solution(12687159146841736572)
XLA Ops:
  0.6 10.8 %shard_map.192 = (f32[4,8,512]{2,1,0:T(8,128)S(1)}, f32[4,8,512]{2,1,0:T(8,128)S(1)}, f32[1,128,128]{2,1,0:T(8,128)S(1)}, f32[1,128,128]{2,1,0:T(8,128)S(1)}) custom-call(f32[4,8,512]{2,1,0:T(8,128)} %refs_0_.1, f32[4,8,512]{2,1,0:T(8,128)} %refs_1_.1, f32[4,8,512]{2,1,0:T(8,128)} %refs_2_.1, f32[4,8,512]{2,1,0:T(8,128)} %refs_3_.1, f32[4,8,512]{2,1,0:T(8,128)} %refs_4_.1, ...), custom_call_target="tpu_custom_call" | custom-call | tf_op jit(solution)/shard_map/pallas_call | solution.py:365
  11.5 0.0 copy-start
  11.5 0.6 %copy-done = f32[4,8,512]{2,1,0:T(8,128)} copy-done((f32[4,8,512]{2,1,0:T(8,128)}, f32[4,8,512]{2,1,0:T(8,128)S(1)}, u32[]{:S(2)}) %copy-start) | copy-done | bytes 65560
  12.1 0.0 copy-start.1
  12.1 0.6 %copy-done.1 = f32[4,8,512]{2,1,0:T(8,128)} copy-done((f32[4,8,512]{2,1,0:T(8,128)}, f32[4,8,512]{2,1,0:T(8,128)S(1)}, u32[]{:S(2)}) %copy-start.1) | copy-done | bytes 65560
  12.7 0.0 copy-start.2
  12.7 0.6 %copy-done.2 = f32[1,128,128]{2,1,0:T(8,128)} copy-done((f32[1,128,128]{2,1,0:T(8,128)}, f32[1,128,128]{2,1,0:T(8,128)S(1)}, u32[]{:S(2)}) %copy-start.2) | copy-done | bytes 65560
  13.4 0.0 copy-start.3
  13.4 0.6 %copy-done.3 = f32[1,128,128]{2,1,0:T(8,128)} copy-done((f32[1,128,128]{2,1,0:T(8,128)}, f32[1,128,128]{2,1,0:T(8,128)S(1)}, u32[]{:S(2)}) %copy-start.3) | copy-done | bytes 65560
  14.0 1.7 %shard_map.193 = (f32[4,8,512]{2,1,0:T(8,128)}, f32[4,8,512]{2,1,0:T(8,128)}, f32[1,128,128]{2,1,0:T(8,128)}, f32[1,128,128]{2,1,0:T(8,128)}) custom-call(f32[4,8,512]{2,1,0:T(8,128)} %copy-done, f32[4,8,512]{2,1,0:T(8,128)} %copy-done.1, f32[1,128,128]{2,1,0:T(8,128)} %copy-done.2, f32[1,128,128]{2,1,0:T(8,128)} %copy-done.3), custom_call_target="tpu_custom_call" | custom-call | tf_op jit(solution)/shard_map/pallas_call | solution.py:386
Async XLA Ops:
  11.5 0.6 %copy-start = (f32[4,8,512]{2,1,0:T(8,128)}, f32[4,8,512]{2,1,0:T(8,128)S(1)}, u32[]{:S(2)}) copy-start(f32[4,8,512]{2,1,0:T(8,128)S(1)} %get-tuple-element.8.refs_0_) | copy-start | bytes 196612
  12.1 0.6 %copy-start.1 = (f32[4,8,512]{2,1,0:T(8,128)}, f32[4,8,512]{2,1,0:T(8,128)S(1)}, u32[]{:S(2)}) copy-start(f32[4,8,512]{2,1,0:T(8,128)S(1)} %get-tuple-element.9.refs_1_) | copy-start | bytes 196612
  12.7 0.6 %copy-start.2 = (f32[1,128,128]{2,1,0:T(8,128)}, f32[1,128,128]{2,1,0:T(8,128)S(1)}, u32[]{:S(2)}) copy-start(f32[1,128,128]{2,1,0:T(8,128)S(1)} %get-tuple-element.10.refs_2_) | copy-start | bytes 196612
  13.4 0.6 %copy-start.3 = (f32[1,128,128]{2,1,0:T(8,128)}, f32[1,128,128]{2,1,0:T(8,128)S(1)}, u32[]{:S(2)}) copy-start(f32[1,128,128]{2,1,0:T(8,128)S(1)} %get-tuple-element.11.refs_3_) | copy-start | bytes 196612
where the time goes:
time: 15.9 us; the launch traced here: 15.6 us
  Pallas kernels  12.5 us (79%)
  local copies, waits for them, and re-layouts  2.49 us (16%)
  between operations  0.66 us (4%)
    pallas_call x1, Pallas kernels, per_device(): pl.pallas_call(functools.partial(kernel, peers), out_shape=outs, in_specs...  10.8 us
    unnamed x8, local copies, waits for them, and re-layouts  2.49 us
    pallas_call x1, Pallas kernels, per_device(): pl.pallas_call(store, out_shape=outs, in_specs=spec(pltpu.VMEM, 4), out_s...  1.66 us

commit v1 on v0

--- a/solution.py
+++ b/solution.py
@@ -117,13 +117,13 @@
 def kernel(peers, *refs):
     ins, outs, scratch = refs[:17], refs[17:21], refs[21:]
     bufs = scratch[:17]
-    send, recv, low, high, load_sem, send_sem, recv_sem, halo_send, halo_recv = scratch[17:]
+    m_ones, f_ones, send, recv, low, high, load_sem, send_sem, recv_sem, halo_send, halo_recv = scratch[17:]
     me = lax.axis_index("strike")
     load = [
         pltpu.make_async_copy(ins[i], bufs[i], load_sem.at[i]) for i in range(17)
     ]
     order = (16, 15, 0, 1, 7, 8, 13, 14, 2, 3, 4, 5, 6, 9, 10, 11, 12)
-    for i in order:
+    for i in order[:8]:
         load[i].start()
 
     barrier = pltpu.get_barrier_semaphore()
@@ -135,6 +135,8 @@
         return carry
 
     lax.fori_loop(1, peers, greet, 0, unroll=peers <= 16)
+    for i in order[8:]:
+        load[i].start()
 
     (press, step, pore, old, t_strike, t_layer, t_dip) = bufs[:7]
     (f_press, f_step, f_volume, f_old, f_along, f_across) = bufs[7:13]
@@ -254,6 +256,9 @@
         load[i].wait()
 
     out_mr, out_mp, out_fr, out_fp = outs
+    m_ones[...] = ones_of(m_row_masks)
+    f_ones[...] = ones_of(f_row_masks)
+
     p, d = press[...], step[...]
     e = jnp.exp(COMPRESSIBILITY * p)
     g = e * d
@@ -331,11 +336,11 @@
         return face(trans, a[0], b[0], a[1], b[1], ea, eb, ea * a[1], eb * b[1])
 
     m_flux, m_tangent = link(got_tr, (mp, md), (got_fp, got_fd))
-    sums = scatter(pack(m_flux), pack(m_tangent), ones_of(m_row_masks), m_col_masks)
+    sums = scatter(pack(m_flux), pack(m_tangent), m_ones[...], m_col_masks)
     out_mr[...] += unfold(sums[0])
     out_mp[...] += unfold(sums[1])
     f_flux, f_tangent = link(tr, (got_mp, got_md), (fp, fd))
-    sums = scatter(pack(f_flux), pack(f_tangent), ones_of(f_row_masks), f_col_masks)
+    sums = scatter(pack(f_flux), pack(f_tangent), f_ones[...], f_col_masks)
     out_fr[0] -= sums[0]
     out_fp[0] -= sums[1]
 
@@ -358,6 +363,7 @@
 
 def per_device(peers, *args):
     nx, nz, ny = args[0].shape
+    slots = peers * args[14].shape[2]
     sems = lambda n: pltpu.SemaphoreType.DMA((n,))
     outs = [jax.ShapeDtypeStruct(args[i].shape, jnp.float32) for i in (0, 0, 7, 7)]
     spec = lambda space, n: [pl.BlockSpec(memory_space=space)] * n
@@ -369,6 +375,8 @@
         out_specs=spec(pltpu.VMEM, 4),
         scratch_shapes=[pltpu.VMEM(x.shape, x.dtype) for x in args]
         + [
+            pltpu.VMEM((nx * nz * ny // LANES, slots), jnp.bfloat16),
+            pltpu.VMEM((args[7].shape[1], slots), jnp.bfloat16),
             pltpu.VMEM((peers, 2, LANES), jnp.float32),
             pltpu.VMEM((peers, 2, LANES), jnp.float32),
             pltpu.VMEM((3, nz, ny), jnp.float32),
@@ -389,6 +397,7 @@
         in_specs=spec(pltpu.VMEM, 4),
         out_specs=spec(pltpu.HBM, 4),
         scratch_shapes=[sems(4)],
+        compiler_params=pltpu.CompilerParams(vmem_limit_bytes=4 * 1024 * 1024),
     )(*results)
 
 

time: 15.9 us -> 12.4 us (0.78)
  local copies, waits for them, and re-layouts: 2.49 us -> 0 us
  Pallas kernels: 12.5 us -> 11.6 us
    unnamed x8 -> x0, local copies, waits for them, and re-layouts: 2.49 us -> none
    pallas_call x1, Pallas kernels: 1.66 us -> 0.73 us  [per_device(): pl.pallas_call(store, out_shape=outs, in_specs=spec(pltpu.VMEM, 4), out_s...]
where the time goes in v1:
time: 12.4 us; the launch traced here: 12.2 us
  Pallas kernels  11.6 us (94%)
  between operations  0.65 us (5%)
    pallas_call x1, Pallas kernels, per_device(): pl.pallas_call(functools.partial(kernel, peers), out_shape=outs, in_specs...  10.8 us
    pallas_call x1, Pallas kernels, per_device(): pl.pallas_call(store, out_shape=outs, in_specs=spec(pltpu.VMEM, 4), out_s...  0.73 us

profile of v1, /device:TPU:0, one launch (start us, length us, event | category | flops | bytes accessed | tf_op | source)
XLA Modules:
  0.0 12.2 jit_solution(16317120799087587273)
XLA Ops:
  0.6 10.8 %shard_map.192 = (f32[4,8,512]{2,1,0:T(8,128)S(1)}, f32[4,8,512]{2,1,0:T(8,128)S(1)}, f32[1,128,128]{2,1,0:T(8,128)S(1)}, f32[1,128,128]{2,1,0:T(8,128)S(1)}) custom-call(f32[4,8,512]{2,1,0:T(8,128)} %refs_0_.1, f32[4,8,512]{2,1,0:T(8,128)} %refs_1_.1, f32[4,8,512]{2,1,0:T(8,128)} %refs_2_.1, f32[4,8,512]{2,1,0:T(8,128)} %refs_3_.1, f32[4,8,512]{2,1,0:T(8,128)} %refs_4_.1, ...), custom_call_target="tpu_custom_call" | custom-call | tf_op jit(solution)/shard_map/pallas_call | solution.py:371
  11.5 0.7 %shard_map.193 = (f32[4,8,512]{2,1,0:T(8,128)}, f32[4,8,512]{2,1,0:T(8,128)}, f32[1,128,128]{2,1,0:T(8,128)}, f32[1,128,128]{2,1,0:T(8,128)}) custom-call(f32[4,8,512]{2,1,0:T(8,128)S(1)} %get-tuple-element.8.refs_0_, f32[4,8,512]{2,1,0:T(8,128)S(1)} %get-tuple-element.9.refs_1_, f32[1,128,128]{2,1,0:T(8,128)S(1)} %get-tuple-element.10.refs_2_, ...), custom_call_target="tpu_custom_call" | custom-call | tf_op jit(solution)/shard_map/pallas_call | solution.py:394

commit v2 on v1

--- a/solution.py
+++ b/solution.py
@@ -64,9 +64,9 @@
 def gather(first, second, row_masks, col_ones):
     size = first.shape[0]
     lhs = jnp.concatenate(
-        [jnp.concatenate(split(x, 3), axis=1) for x in (first, second)], axis=0
-    )
-    rhs = jnp.concatenate([col_ones] * 3, axis=0)
+        [jnp.concatenate(split(x, 2), axis=1) for x in (first, second)], axis=0
+    )
+    rhs = jnp.concatenate([col_ones] * 2, axis=0)
     found = jnp.dot(lhs, rhs, preferred_element_type=jnp.float32)
     out = []
     for q in range(2):
@@ -119,6 +119,10 @@
     bufs = scratch[:17]
     m_ones, f_ones, send, recv, low, high, load_sem, send_sem, recv_sem, halo_send, halo_recv = scratch[17:]
     me = lax.axis_index("strike")
+
+    def wrap(x):
+        return jnp.where(x >= peers, x - peers, x)
+
     load = [
         pltpu.make_async_copy(ins[i], bufs[i], load_sem.at[i]) for i in range(17)
     ]
@@ -130,14 +134,11 @@
 
     def greet(off, carry):
         pl.semaphore_signal(
-            barrier, 1, device_id={"strike": lax.rem(me + off, peers)}, device_id_type=MESH
+            barrier, 1, device_id={"strike": wrap(me + off)}, device_id_type=MESH
         )
         return carry
 
     lax.fori_loop(1, peers, greet, 0, unroll=peers <= 16)
-    for i in order[8:]:
-        load[i].start()
-
     (press, step, pore, old, t_strike, t_layer, t_dip) = bufs[:7]
     (f_press, f_step, f_volume, f_old, f_along, f_across) = bufs[7:13]
     count, c_trans, f_index, m_index = bufs[13:]
@@ -159,7 +160,7 @@
         )
         return flat.reshape(nx, nz, ny)
 
-    for i in (16, 0, 1):
+    for i in order[:8]:
         load[i].wait()
     cell = pack(m_index[0])
     along = cell & (ny - 1)
@@ -170,8 +171,6 @@
     mp, md = gather(fold(press[...]), fold(step[...]), m_row_masks, ones_of(m_col_masks))
     mp, md = unpack(mp, cap), unpack(md, cap)
 
-    for i in (15, 7, 8):
-        load[i].wait()
     cell = pack(f_index[0])
     f_row = cell >> 7
     f_col = cell & (LANES - 1)
@@ -180,8 +179,6 @@
     fp, fd = gather(f_press[0], f_step[0], f_row_masks, ones_of(f_col_masks))
     fp, fd = unpack(fp, cap), unpack(fd, cap)
 
-    for i in (13, 14):
-        load[i].wait()
     diagonal = lax.broadcasted_iota(jnp.int32, (peers, peers), 0) == lax.broadcasted_iota(
         jnp.int32, (peers, peers), 1
     )
@@ -201,20 +198,23 @@
         return pltpu.make_async_remote_copy(
             src_ref=send.at[to],
             dst_ref=recv.at[slot_there],
-            send_sem=send_sem.at[off],
-            recv_sem=recv_sem.at[off],
+            send_sem=send_sem.at[0],
+            recv_sem=recv_sem.at[0],
             device_id={"strike": to},
             device_id_type=MESH,
         )
 
     def push(off, carry):
-        exchange(off, lax.rem(me + off, peers), me).start()
+        exchange(off, wrap(me + off), me).start()
         return carry
 
     lax.fori_loop(1, peers, push, 0, unroll=peers <= 16)
 
-    following = lax.rem(me + 1, peers)
-    previous = lax.rem(me + peers - 1, peers)
+    for i in order[8:]:
+        load[i].start()
+
+    following = wrap(me + 1)
+    previous = wrap(me + peers - 1)
 
     load[4].wait()
     upward = [
@@ -250,6 +250,14 @@
         for copy in downward:
             copy.start()
 
+    everything = pltpu.make_async_remote_copy(
+        src_ref=send.at[pl.ds(0, peers - 1)],
+        dst_ref=recv.at[pl.ds(0, peers - 1)],
+        send_sem=send_sem.at[0],
+        recv_sem=recv_sem.at[0],
+        device_id={"strike": following},
+        device_id_type=MESH,
+    )
     recv[me] = send[me]
 
     for i in (2, 3, 5, 6, 9, 10, 11, 12):
@@ -321,11 +329,7 @@
         out_mr[nx - 1] = out_mr[nx - 1] + flux
         out_mp[nx - 1] = out_mp[nx - 1] + tangent
 
-    def take(off, carry):
-        exchange(off, lax.rem(me + off, peers), lax.rem(me + peers - off, peers)).wait_recv()
-        return carry
-
-    lax.fori_loop(1, peers, take, 0, unroll=peers <= 16)
+    everything.wait_recv()
 
     got = recv[:, 0, :]
     got_fp, got_fd, got_tr, got_mp = (got[:, i * cap : (i + 1) * cap] for i in range(4))
@@ -344,11 +348,7 @@
     out_fr[0] -= sums[0]
     out_fp[0] -= sums[1]
 
-    def sent(off, carry):
-        exchange(off, lax.rem(me + off, peers), me).wait_send()
-        return carry
-
-    lax.fori_loop(1, peers, sent, 0, unroll=peers <= 16)
+    everything.wait_send()
 
     @pl.when(me < peers - 1)
     def _():
@@ -382,8 +382,8 @@
             pltpu.VMEM((3, nz, ny), jnp.float32),
             pltpu.VMEM((2, nz, ny), jnp.float32),
             sems(17),
-            sems(peers),
-            sems(peers),
+            sems(1),
+            sems(1),
             sems(5),
             sems(5),
         ],

time: 12.4 us -> 11.6 us (0.935)
  Pallas kernels: 11.6 us -> 10.8 us
    pallas_call x1, Pallas kernels: 10.8 us -> 10 us  [per_device(): pl.pallas_call(functools.partial(kernel, peers), out_shape=outs, in_specs...]
where the time goes in v2:
time: 11.6 us; the launch traced here: 11.4 us
  Pallas kernels  10.8 us (93%)
  between operations  0.65 us (6%)
    pallas_call x1, Pallas kernels, per_device(): pl.pallas_call(functools.partial(kernel, peers), out_shape=outs, in_specs...  10 us
    pallas_call x1, Pallas kernels, per_device(): pl.pallas_call(store, out_shape=outs, in_specs=spec(pltpu.VMEM, 4), out_s...  0.73 us

profile of v2, /device:TPU:0, one launch (start us, length us, event | category | flops | bytes accessed | tf_op | source)
XLA Modules:
  0.0 11.4 jit_solution(849327284687970368)
XLA Ops:
  0.6 10.0 %shard_map.192 = (f32[4,8,512]{2,1,0:T(8,128)S(1)}, f32[4,8,512]{2,1,0:T(8,128)S(1)}, f32[1,128,128]{2,1,0:T(8,128)S(1)}, f32[1,128,128]{2,1,0:T(8,128)S(1)}) custom-call(f32[4,8,512]{2,1,0:T(8,128)} %refs_0_.1, f32[4,8,512]{2,1,0:T(8,128)} %refs_1_.1, f32[4,8,512]{2,1,0:T(8,128)} %refs_2_.1, f32[4,8,512]{2,1,0:T(8,128)} %refs_3_.1, f32[4,8,512]{2,1,0:T(8,128)} %refs_4_.1, ...), custom_call_target="tpu_custom_call" | custom-call | tf_op jit(solution)/shard_map/pallas_call | solution.py:371
  10.7 0.7 %shard_map.193 = (f32[4,8,512]{2,1,0:T(8,128)}, f32[4,8,512]{2,1,0:T(8,128)}, f32[1,128,128]{2,1,0:T(8,128)}, f32[1,128,128]{2,1,0:T(8,128)}) custom-call(f32[4,8,512]{2,1,0:T(8,128)S(1)} %get-tuple-element.8.refs_0_, f32[4,8,512]{2,1,0:T(8,128)S(1)} %get-tuple-element.9.refs_1_, f32[1,128,128]{2,1,0:T(8,128)S(1)} %get-tuple-element.10.refs_2_, ...), custom_call_target="tpu_custom_call" | custom-call | tf_op jit(solution)/shard_map/pallas_call | solution.py:394
